TPU v7x, 32 devices: a whole 2x2x4 slice. The times are simulated.
32 devices in a mesh: groups: 2 (over y), ra: 4 (over z), dec: 2 (over x), band: 2 (over core).
Axes of the slice: x: 2, y: 2, z: 4, core: 2. Of those that a mesh axis runs over, the one named last changes fastest.
Arguments:
- sky_maps: bfloat16 [512, 312, 256], P(('groups', 'band'), 'ra', 'dec'), parts along dimension 0, may hold values from -12 to 12
- radii: int32 [512], P(('groups', 'band')), parts along dimension 0, may hold values from 1 to 17, as said below
- valid: int32 [624, 256], P(('groups', 'ra'), 'dec'), parts along dimension 0, may hold values from 0 to 1, as said below
Outputs:
- smoothed: bfloat16 [512, 312, 256], P(('groups', 'band'), 'ra', 'dec'), parts along dimension 0
- channel_mean: float32 [512], P(('groups', 'band')), parts along dimension 0
- covariance: float32 [512, 256], P('groups', 'band'), parts along dimension 0
There are 2 independent parts, one for each index of `groups`. A program takes and returns all parts, laid end to end along the dimension named above; each array names one. Nothing has to cross between parts.
Inputs may be any that keep to these rules, and one draw needn't show every extreme that they name: `radii`: some channel has half-width exactly 17. 1 marks a pixel that enters the statistics; the pixel with declination index 0 is valid in every row.
All inputs are finite; a program needn't handle non-finite values.
Results may differ from a plain program's by a relative error of at most 0.012.
The roundings to bfloat16 on the way count: a program that leaves them out, or rounds other values in their place, can miss the bound.
Values may be sent and summed in bfloat16 or wider, within the bound.
A program may use at most 64 MiB of HBM per device.

v0:
```python
import jax
import jax.numpy as jnp
from jax import lax
from jax.sharding import PartitionSpec as P

RMAX = 17


def extended(array, sides, width, wrap):
    for axis, dim in sides:
        peers, length = (lax.axis_size(axis), array.shape[dim])
        up = [(i, (i + 1) % peers) for i in range(peers if wrap else peers - 1)]
        down = [(j, i) for i, j in up]
        last = lax.slice_in_dim(array, length - width, length, axis=dim)
        initial = lax.slice_in_dim(array, 0, width, axis=dim)
        before = lax.ppermute(last, axis, up)
        after = lax.ppermute(initial, axis, down)
        array = jnp.concatenate([before, array, after], axis=dim)
    return array


def beam_taps(radii, offsets):
    radius = radii.astype(jnp.float32)
    lead_shape = (radii.shape[0],) + (1,) * offsets.ndim
    radius = radius.reshape(lead_shape)
    spread = 0.5 * radius
    inside = jnp.abs(offsets)[None] <= radius
    return jnp.where(inside, jnp.exp(-(offsets * offsets)[None] / (2.0 * spread * spread)), 0.0)


def banded(radii, inner_count, outer_count):
    raw_taps = beam_taps(radii, jnp.arange(-RMAX, RMAX + 1).astype(jnp.float32))
    tap_total = jnp.sum(raw_taps, axis=1)
    offsets = (
        lax.broadcasted_iota(jnp.int32, (inner_count, outer_count), 0)
        - lax.broadcasted_iota(jnp.int32, (inner_count, outer_count), 1)
        - RMAX
    ).astype(jnp.float32)
    return (beam_taps(radii, offsets) / tap_total[:, None, None]).astype(jnp.bfloat16)


def local_sums(maps, mask_values):
    flat = maps.reshape(maps.shape[0], -1)
    weights = mask_values.reshape(-1)
    masked = flat * weights.astype(jnp.bfloat16)[None]
    sums = jnp.sum(masked.astype(jnp.float32), axis=1)
    return (masked, sums, jnp.sum(weights))


def per_device(sky_maps, radii, valid):
    channel_count, pixel_rows, pixel_cols = sky_maps.shape
    dec_band = banded(radii, pixel_cols + 2 * RMAX, pixel_cols)
    ra_band = banded(radii, pixel_rows + 2 * RMAX, pixel_rows)
    wrapped = extended(sky_maps, (("ra", 1),), RMAX, True)
    framed = extended(wrapped, (("dec", 2),), RMAX, False)
    across = jnp.einsum(
        "cxz,czy->cxy", framed, dec_band, preferred_element_type=jnp.float32
    ).astype(jnp.bfloat16)
    smoothed = jnp.einsum(
        "czy,czw->cwy", across, ra_band, preferred_element_type=jnp.float32
    ).astype(jnp.bfloat16)
    mask_values = valid.astype(jnp.float32)
    first_channel = lax.axis_index("band") * channel_count
    every = lax.all_gather(smoothed, "band", axis=0, tiled=True)
    masked, sums, count = local_sums(every, mask_values)
    own_rows = lax.dynamic_slice_in_dim(masked, first_channel, channel_count, 0)
    block = lax.dot_general(
        masked, own_rows, (((1,), (1,)), ((), ())), preferred_element_type=jnp.float32
    )
    sums, count, block = lax.psum((sums, count, block), ("ra", "dec"))
    mean_all = sums / count
    channel_mean = lax.dynamic_slice_in_dim(mean_all, first_channel, channel_count, 0)
    covariance = (block - count * mean_all[:, None] * channel_mean[None, :]) / (count - 1.0)
    return (smoothed, channel_mean, covariance)


def solution(mesh):
    return jax.shard_map(
        per_device,
        mesh=mesh,
        in_specs=(
            P(("groups", "band"), "ra", "dec"),
            P(("groups", "band")),
            P(("groups", "ra"), "dec"),
        ),
        out_specs=(P(("groups", "band"), "ra", "dec"), P(("groups", "band")), P("groups", "band")),
        check_vma=False,
    )
```

profile of v0, /device:TPU:0, one launch (start us, length us, event | category | flops | bytes accessed | tf_op | source)
XLA Modules:
  0.0 190.9 jit_solution(9157227778549513392)
XLA Ops:
  7.2 1.3 fusion.54
  8.5 3.1 %collective-permute-start = (bf16[128,17,128]{2,0,1:T(8,128)(2,1)S(1)}, bf16[128,17,128]{2,0,1:T(8,128)(2,1)S(1)}, u32[]{:S(2)}, u32[]{:S(2)}) collective-permute-start(bf16[128,17,128]{2,0,1:T(8,128)(2,1)S(1)} %get-tuple-element.24), channel_id=1, source_target_pairs={{0,4},{4,8},{8,12},{12,0},{1,5},{5,9},{9,13},{13,1},{2,6},{6,10},{... | collective-permute-start | bytes 1671176 | tf_op jit(solution)/shard_map/ppermute | solution.py:16
  11.6 2.1 %collective-permute-start.1 = (bf16[128,17,128]{2,0,1:T(8,128)(2,1)S(1)}, bf16[128,17,128]{2,0,1:T(8,128)(2,1)S(1)}, u32[]{:S(2)}, u32[]{:S(2)}) collective-permute-start(bf16[128,17,128]{2,0,1:T(8,128)(2,1)S(1)} %get-tuple-element.25), channel_id=1, source_target_pairs={{4,0},{8,4},{12,8},{0,12},{5,1},{9,5},{13,9},{1,13},{6,2},{10,6},{... | collective-permute-start | bytes 1671176 | tf_op jit(solution)/shard_map/ppermute | solution.py:17
  13.7 6.1 %copy.30 = bf16[128,78,128]{1,2,0:T(8,128)(2,1)} copy(bf16[128,78,128]{2,0,1:T(8,128)(2,1)} %param.3) | data formatting | bytes 5111808 | tf_op args[0]
  19.8 0.6 multiply_negate_fusion.1
  20.5 6.7 %collective-permute-done = bf16[128,17,128]{2,0,1:T(8,128)(2,1)S(1)} collective-permute-done((bf16[128,17,128]{2,0,1:T(8,128)(2,1)S(1)}, bf16[128,17,128]{2,0,1:T(8,128)(2,1)S(1)}, u32[]{:S(2)}, u32[]{:S(2)}) %collective-permute-start) | collective-permute-done | bytes 557088 | tf_op jit(solution)/shard_map/ppermute | solution.py:16
  27.1 3.3 %copy.29 = bf16[128,17,128]{1,2,0:T(8,128)(2,1)} copy(bf16[128,17,128]{2,0,1:T(8,128)(2,1)S(1)} %collective-permute-done) | data formatting | bytes 1114112 | tf_op jit(solution)/shard_map/ppermute | solution.py:16
  30.4 7.2 %collective-permute-done.1 = bf16[128,17,128]{2,0,1:T(8,128)(2,1)S(1)} collective-permute-done((bf16[128,17,128]{2,0,1:T(8,128)(2,1)S(1)}, bf16[128,17,128]{2,0,1:T(8,128)(2,1)S(1)}, u32[]{:S(2)}, u32[]{:S(2)}) %collective-permute-start.1) | collective-permute-done | bytes 557088 | tf_op jit(solution)/shard_map/ppermute | solution.py:17
  37.6 3.3 %copy.31 = bf16[128,17,128]{1,2,0:T(8,128)(2,1)} copy(bf16[128,17,128]{2,0,1:T(8,128)(2,1)S(1)} %collective-permute-done.1) | data formatting | bytes 1114112 | tf_op jit(solution)/shard_map/ppermute | solution.py:17
  40.9 4.2 %pad_maximum_fusion.2 = (bf16[128,112,17]{1,2,0:T(8,128)(2,1)S(1)}, bf16[128,112,17]{1,2,0:T(8,128)(2,1)S(1)}) fusion(bf16[128,17,128]{1,2,0:T(8,128)(2,1)} %copy.31, bf16[128,78,128]{1,2,0:T(8,128)(2,1)} %copy.30, bf16[128,17,128]{1,2,0:T(8,128)(2,1)} %copy.29), kind=kLoop, calls=%fused_computation.39 | loop fusion | flops 2924544 | bytes 4644864 | tf_op jit(solution)/shard_map/slice | solution.py:14
  45.1 0.5 copy.32
  45.5 3.4 %collective-permute-start.2 = (bf16[128,112,17]{0,1,2:T(8,128)(2,1)S(1)}, bf16[128,112,17]{0,1,2:T(8,128)(2,1)S(1)}, u32[]{:S(2)}, u32[]{:S(2)}) collective-permute-start(bf16[128,112,17]{0,1,2:T(8,128)(2,1)S(1)} %copy.32), channel_id=1, source_target_pairs={{0,2},{1,3},{4,6},{5,7},{8,10},{9,11},{12,14},{13,15},{16,18},{17,... | collective-permute-start | bytes 1462280 | tf_op jit(solution)/shard_map/ppermute | solution.py:16
  49.0 0.5 copy.33
  49.4 1.3 collective-permute-start.3
  50.9 0.7 multiply_negate_fusion
  51.5 7.3 %collective-permute-done.2 = bf16[128,112,17]{0,1,2:T(8,128)(2,1)S(1)} collective-permute-done((bf16[128,112,17]{0,1,2:T(8,128)(2,1)S(1)}, bf16[128,112,17]{0,1,2:T(8,128)(2,1)S(1)}, u32[]{:S(2)}, u32[]{:S(2)}) %collective-permute-start.2) | collective-permute-done | bytes 487456 | tf_op jit(solution)/shard_map/ppermute | solution.py:16
  58.9 0.4 copy.34
  59.3 4.2 %collective-permute-done.3 = bf16[128,112,17]{0,1,2:T(8,128)(2,1)S(1)} collective-permute-done((bf16[128,112,17]{0,1,2:T(8,128)(2,1)S(1)}, bf16[128,112,17]{0,1,2:T(8,128)(2,1)S(1)}, u32[]{:S(2)}, u32[]{:S(2)}) %collective-permute-start.3) | collective-permute-done | bytes 487456 | tf_op jit(solution)/shard_map/ppermute | solution.py:17
  63.5 1.2 copy.35
  64.7 13.9 %fusion.34 = bf16[128,78,128]{2,1,0:T(8,128)(2,1)S(1)} fusion(f32[128]{0:T(128)S(1)} %fusion.48, f32[128]{0:T(128)S(1)} %multiply_multiply_fusion, f32[112,78]{0,1:T(8,128)S(1)} %get-tuple-element.30, f32[112,78]{0,1:T(8,128)} %get-tuple-element.31, f32[128]{0:T(128)S(1)} %convert_element_type.74, bf16[128,112,17]{1,2,0:T(8,128)(2,1)} %copy.35, ...), kind=kOutput, calls=%fused_computation.36 | convolution fusion | flops 926003200 | bytes 7438080 | tf_op jit(solution)/shard_map/czy,czw->cwy/dot_general | solution.py:59
  78.7 2.1 %copy.38 = bf16[128,78,128]{2,0,1:T(8,128)(2,1)} copy(bf16[128,78,128]{2,1,0:T(8,128)(2,1)S(1)} %fusion.34) | data formatting | bytes 5111808
  80.9 0.2 all-reduce.3.cloned.1.call-start
  81.1 0.6 convert_reduce_fusion.1
  81.7 13.3 %all-gather.2.cloned.1.call-done = bf16[256,78,128]{2,0,1:T(8,128)(2,1)} async-done(((bf16[128,78,128]{2,0,1:T(8,128)(2,1)}), bf16[256,78,128]{2,0,1:T(8,128)(2,1)}) %all-gather.2.cloned.1.call-update) | async-done | bytes 5111824 | tf_op jit(solution)/shard_map/all_gather | solution.py:64
  95.0 7.7 %copy.37 = bf16[256,78,128]{0,2,1:T(8,128)(2,1)} copy(bf16[256,78,128]{2,0,1:T(8,128)(2,1)} %all-gather.2.cloned.1.call-done) | data formatting | bytes 10223616 | tf_op jit(solution)/shard_map/all_gather | solution.py:64
  102.8 6.3 %bitcast_multiply_fusion = bf16[256,9984]{0,1:T(8,128)(2,1)S(1)} fusion(bf16[256,78,128]{0,2,1:T(8,128)(2,1)} %copy.37, bf16[9984]{0:T(1024)(128)(2,1)S(1)} %fusion.56), kind=kLoop, calls=%fused_computation.25 | loop fusion | flops 2555904 | bytes 10243584 | tf_op jit(solution)/shard_map/mul | solution.py:45
  109.0 2.3 %fusion.32 = f32[256,128]{1,0:T(8,128)} fusion(bf16[256,9984]{0,1:T(8,128)(2,1)S(1)} %bitcast_multiply_fusion, s32[]{:T(128)S(6)} %select_n.20), kind=kOutput, calls=%fused_computation.34 | convolution fusion | flops 654311424 | bytes 7798788 | tf_op jit(solution)/shard_map/dot_general | solution.py:67
  111.3 3.7 %convert_reduce_fusion = f32[256]{0:T(256)S(1)} fusion(bf16[256,78,128]{2,0,1:T(8,128)(2,1)} %all-gather.2.cloned.1.call-done, bf16[78,128]{1,0:T(8,128)(2,1)S(1)} %convert_convert_fusion), kind=kLoop, calls=%fused_computation.4 | loop fusion | flops 7667456 | bytes 5132800 | tf_op jit(solution)/shard_map/reduce_sum | solution.py:46
  115.0 22.4 %all-reduce = (f32[256]{0:T(256)S(1)}, f32[]{:T(128)}) all-reduce(f32[256]{0:T(256)S(1)} %convert_reduce_fusion, f32[]{:T(128)} %convert_reduce_fusion.1), channel_id=1, replica_groups=mesh['groups'=2,'ra'=4,'dec'=2,'band'=2] {'ra','dec'}, use_global_device_ids=true, to_apply=%region_2.3 | all-reduce | flops 257 | bytes 2056 | tf_op jit(solution)/shard_map/psum | solution.py:70
  137.4 0.6 broadcast_multiply_fusion
  138.6 43.8 %all-reduce.3.cloned.1.call-done = f32[256,128]{1,0:T(8,128)} async-done(((f32[256,128]{1,0:T(8,128)}), f32[256,128]{1,0:T(8,128)}) %all-reduce.3.cloned.1.call-update) | async-done | bytes 131088 | tf_op jit(solution)/shard_map/psum | solution.py:70
  182.3 1.7 subtract_divide_fusion
  (16 shorter events, 0.3 us)
Async XLA Ops:
  7.2 87.9 %all-gather.2.cloned.1.call-start = ((), (), s32[]{:S(2)}) async-start(), calls=%async_computation | async-start | bytes 7667712 | tf_op jit(solution)/shard_map/all_gather | solution.py:64
  8.5 18.6 %collective-permute-start = (bf16[128,17,128]{2,0,1:T(8,128)(2,1)S(1)}, bf16[128,17,128]{2,0,1:T(8,128)(2,1)S(1)}, u32[]{:S(2)}, u32[]{:S(2)}) collective-permute-start(bf16[128,17,128]{2,0,1:T(8,128)(2,1)S(1)} %get-tuple-element.24), channel_id=1, source_target_pairs={{0,4},{4,8},{8,12},{12,0},{1,5},{5,9},{9,13},{13,1},{2,6},{6,10},{... | collective-permute-start | bytes 1671176 | tf_op jit(solution)/shard_map/ppermute | solution.py:16
  11.6 26.0 %collective-permute-start.1 = (bf16[128,17,128]{2,0,1:T(8,128)(2,1)S(1)}, bf16[128,17,128]{2,0,1:T(8,128)(2,1)S(1)}, u32[]{:S(2)}, u32[]{:S(2)}) collective-permute-start(bf16[128,17,128]{2,0,1:T(8,128)(2,1)S(1)} %get-tuple-element.25), channel_id=1, source_target_pairs={{4,0},{8,4},{12,8},{0,12},{5,1},{9,5},{13,9},{1,13},{6,2},{10,6},{... | collective-permute-start | bytes 1671176 | tf_op jit(solution)/shard_map/ppermute | solution.py:17
  40.9 9.9 %copy-start.2 = (s32[128]{0:T(128)S(1)}, s32[128]{0:T(128)}, u32[]{:S(2)}) copy-start(s32[128]{0:T(128)} %param.4) | copy-start | bytes 1540
  45.5 13.3 %collective-permute-start.2 = (bf16[128,112,17]{0,1,2:T(8,128)(2,1)S(1)}, bf16[128,112,17]{0,1,2:T(8,128)(2,1)S(1)}, u32[]{:S(2)}, u32[]{:S(2)}) collective-permute-start(bf16[128,112,17]{0,1,2:T(8,128)(2,1)S(1)} %copy.32), channel_id=1, source_target_pairs={{0,2},{1,3},{4,6},{5,7},{8,10},{9,11},{12,14},{13,15},{16,18},{17,... | collective-permute-start | bytes 1462280 | tf_op jit(solution)/shard_map/ppermute | solution.py:16
  49.4 14.0 %collective-permute-start.3 = (bf16[128,112,17]{0,1,2:T(8,128)(2,1)S(1)}, bf16[128,112,17]{0,1,2:T(8,128)(2,1)S(1)}, u32[]{:S(2)}, u32[]{:S(2)}) collective-permute-start(bf16[128,112,17]{0,1,2:T(8,128)(2,1)S(1)} %copy.33), channel_id=1, source_target_pairs={{2,0},{3,1},{6,4},{7,5},{10,8},{11,9},{14,12},{15,13},{18,16},{19,... | collective-permute-start | bytes 1462280 | tf_op jit(solution)/shard_map/ppermute | solution.py:17
  78.7 2.4 %copy-start = (s32[78,128]{1,0:T(8,128)S(1)}, s32[78,128]{1,0:T(8,128)}, u32[]{:S(2)}) copy-start(s32[78,128]{1,0:T(8,128)} %param.5) | copy-start | bytes 119812
  80.9 101.5 %all-reduce.3.cloned.1.call-start = ((), (), s32[]{:S(2)}) async-start(), calls=%async_computation.1 | async-start | bytes 262144 | tf_op jit(solution)/shard_map/psum | solution.py:70
  138.0 46.0 %copy-start.1 = (f32[128]{0:T(128)}, f32[128]{0:T(128)S(1)}, u32[]{:S(2)}) copy-start(f32[128]{0:T(128)S(1)} %dynamic_slice.6) | copy-start | bytes 1540
Sparse Core Ops, SparseCore 0:
  81.0 13.9 all-gather.1
  111.4 70.8 all-reduce.2
where the time goes:
time: 191 us
  waiting for transfers between devices  82.4 us (43%)
  local copies, waits for them, and re-layouts  26.6 us (14%)
  blocking collectives  22.4 us (12%)
  other arithmetic  18.3 us (10%)
  matrix products  16.2 us (8%)
  between operations  14.7 us (8%)
  starting transfers between devices  10.1 us (5%)
    psum x1, waiting for transfers between devices, per_device(): sums, count, block = lax.psum((sums, count, block), ('ra', 'dec'))  43.8 us
    psum x1, blocking collectives, per_device(): sums, count, block = lax.psum((sums, count, block), ('ra', 'dec'))  22.4 us
    ppermute x2, waiting for transfers between devices, extended(): before = lax.ppermute(last, axis, up)  14 us
    dot_general x1, matrix products, per_device(): jnp.einsum('czy,czw->cwy', across, ra_band, preferred_element_type=jnp.fl...  13.9 us
    all_gather x1, waiting for transfers between devices, per_device(): every = lax.all_gather(smoothed, 'band', axis=0, tiled=True)  13.3 us
    ppermute x2, waiting for transfers between devices, extended(): after = lax.ppermute(initial, axis, down)  11.4 us
    unnamed x8, local copies, waits for them, and re-layouts  8.3 us
    all_gather x1, local copies, waits for them, and re-layouts, per_device(): every = lax.all_gather(smoothed, 'band', axis=0, tiled=True)  7.73 us
  transfers between devices with their start and end apart: 6, of which 6 were waited for; matrix products, arithmetic and copies ran while one was open for 9% of the time, Pallas kernels for 0%

commit v1 on v0

v1 whole, which is shorter than its diff:
```python
import functools

import jax
import jax.numpy as jnp
from jax import lax
from jax.experimental import pallas as pl
from jax.experimental.pallas import tpu as pltpu
from jax.sharding import PartitionSpec as P

RMAX = 17
WIDE = RMAX + 1
CB = 16
MESH = pl.DeviceIdType.MESH


def up(value, step):
    return -(-value // step) * step


def iota(shape, dim):
    return lax.broadcasted_iota(jnp.int32, shape, dim)


def kernel(
    dims, radii_ref, sky_ref, valid_ref, out_ref, mean_ref, cov_ref,
    tab_dec, tab_ra, xs, hs, os, ps, vb, mine, other,
    pack_up, pack_dn, halo_lo, halo_hi, edge_lo, edge_hi, z_before, z_after,
    acc, shares, total, aux, aux_all,
    s_dec, r_dec, s_ra, r_ra, s_band, r_band, s_rs, r_rs, s_ag, r_ag, s_aux, r_aux,
):
    n_ra, n_dec, rows, chans, cols = dims
    blocks = chans // CB
    rows8 = up(rows, 16)
    groups = cols // WIDE
    per = -(-rows // groups)
    peers = n_ra * n_dec
    reducers = min(peers, chans // 8)
    share = chans // reducers
    ext = 128
    ra, dec, band = lax.axis_index("ra"), lax.axis_index("dec"), lax.axis_index("band")
    rank = ra * n_dec + dec
    nxt, prv = lax.rem(ra + 1, n_ra), lax.rem(ra + n_ra - 1, n_ra)
    twin = {"band": 1 - band}

    def peer_id(p):
        return {"ra": p // n_dec, "dec": lax.rem(p, n_dec)}

    def each_peer(body):
        def step(d, carry):
            body(lax.rem(rank + d, peers))
            return carry
        lax.fori_loop(1, peers, step, 0)

    barrier = pltpu.get_barrier_semaphore()
    each_peer(lambda p: pl.semaphore_signal(barrier, inc=1, device_id=peer_id(p), device_id_type=MESH))
    pl.semaphore_signal(barrier, inc=1, device_id=twin, device_id_type=MESH)
    pl.semaphore_wait(barrier, peers)

    def remote(src, dst, send, recv, target):
        return pltpu.make_async_remote_copy(
            src_ref=src, dst_ref=dst, send_sem=send, recv_sem=recv, device_id=target, device_id_type=MESH
        )

    def dec_up(b):
        return remote(pack_up.at[b], halo_lo.at[b], s_dec.at[0, b], r_dec.at[0, b], {"dec": dec + 1})

    def dec_dn(b):
        return remote(pack_dn.at[b], halo_hi.at[b], s_dec.at[1, b], r_dec.at[1, b], {"dec": dec - 1})

    def ra_up(b):
        return remote(edge_hi.at[b], z_before.at[b], s_ra.at[0, b], r_ra.at[0, b], {"ra": nxt})

    def ra_dn(b):
        return remote(edge_lo.at[b], z_after.at[b], s_ra.at[1, b], r_ra.at[1, b], {"ra": prv})

    def to_twin(b):
        return remote(mine.at[b], other.at[b], s_band.at[b], r_band.at[b], twin)

    has_hi, has_lo = dec < n_dec - 1, dec > 0
    lanes = iota((1, 1, cols), 2)
    tall = per * groups
    xs[...] = jnp.zeros_like(xs)

    def load_block(b):
        at = pl.multiple_of(b * CB, CB)
        block = sky_ref[:, pl.ds(at, CB), :].astype(jnp.float32)
        xs[0:rows * CB, :] = block.reshape(rows * CB, cols)

    def pack_block(b, carry):
        load_block(b)

        def packed(first):
            result = jnp.zeros((per, CB, cols), jnp.float32)
            for g in range(groups):
                part = xs[g * per * CB:(g + 1) * per * CB, :].reshape(per, CB, cols)
                turned = pltpu.roll(part, (WIDE * g - first) % cols, 2)
                inside = (lanes >= WIDE * g) & (lanes < WIDE * (g + 1))
                result = jnp.where(inside, turned, result)
            return result.astype(jnp.bfloat16)

        @pl.when(has_hi)
        def _():
            pack_up[b] = packed(cols - WIDE)
            dec_up(b).start()

        @pl.when(has_lo)
        def _():
            pack_dn[b] = packed(0)
            dec_dn(b).start()

        return carry

    lax.fori_loop(0, blocks, pack_block, 0)

    def table(r, carry):
        radius = r.astype(jnp.float32)
        spread = 0.5 * radius

        def taps(k):
            k = k.astype(jnp.float32)
            return jnp.where(jnp.abs(k) <= radius, jnp.exp(-(k * k) / (2.0 * spread * spread)), 0.0)

        norm = jnp.sum(taps(iota((1, 128), 1) - 64), axis=1, keepdims=True)
        z, y = iota((cols, cols), 0), iota((cols, cols), 1)
        tab_dec[r, 0:cols, :] = (taps(z - y) / norm).astype(jnp.bfloat16)
        j = jnp.where(z < WIDE, cols + z, jnp.where((z >= 64) & (z < 64 + WIDE), z - 64 - WIDE, 4 * cols))
        tab_dec[r, cols:2 * cols, :] = (taps(j - y) / norm).astype(jnp.bfloat16)
        x, e = iota((rows8, ext), 0), iota((rows8, ext), 1)
        at = jnp.where(
            e < rows, e,
            jnp.where(
                (e >= rows8) & (e < rows8 + RMAX), e - rows8 - RMAX,
                jnp.where((e >= rows8 + RMAX) & (e < rows8 + 2 * RMAX), e - rows8 - RMAX + rows, 4 * ext),
            ),
        )
        tab_ra[r] = (taps(at - x) / norm).astype(jnp.bfloat16)
        return carry

    lax.fori_loop(1, RMAX + 1, table, 0)

    used = rows8 + 2 * RMAX

    @pl.when(jnp.logical_not(has_lo))
    def _():
        halo_lo[...] = jnp.zeros_like(halo_lo)

    @pl.when(jnp.logical_not(has_hi))
    def _():
        halo_hi[...] = jnp.zeros_like(halo_hi)

    def dec_block(b, carry):
        load_block(b)
        ps[b, used * CB:ext * CB, :] = jnp.zeros(((ext - used) * CB, cols), jnp.float32)

        @pl.when(has_lo)
        def _():
            dec_up(b).wait_recv()

        @pl.when(has_hi)
        def _():
            dec_dn(b).wait_recv()

        low = halo_lo[b].astype(jnp.float32)
        high = halo_hi[b].astype(jnp.float32)
        for g in range(groups):
            left = pltpu.roll(low, (64 - WIDE * g) % cols, 2)
            right = pltpu.roll(high, (-WIDE * g) % cols, 2)
            both = jnp.where(lanes < 64, right, left)
            hs[g * per * CB:(g + 1) * per * CB, :] = both.reshape(per * CB, cols)
        for c in range(CB):
            rr = radii_ref[b * CB + c]
            main = xs[pl.ds(c, rows8, stride=CB), :]
            side = hs[pl.ds(c, rows8, stride=CB), :]
            left_hand = jnp.concatenate([main, side], axis=1).astype(jnp.bfloat16)
            part = jnp.dot(left_hand, tab_dec[rr], preferred_element_type=jnp.float32)
            part = part.astype(jnp.bfloat16).astype(jnp.float32)
            ps[b, pl.ds(c, rows8, stride=CB), :] = part
        edge_lo[b] = ps[b, 0:RMAX * CB, :].reshape(RMAX, CB, cols).astype(jnp.bfloat16)
        last = ps[b, (rows - RMAX) * CB:rows * CB, :]
        edge_hi[b] = last.reshape(RMAX, CB, cols).astype(jnp.bfloat16)
        ra_up(b).start()
        ra_dn(b).start()
        return carry

    lax.fori_loop(0, blocks, dec_block, 0)

    weights = valid_ref[...].astype(jnp.float32)
    for x in range(rows):
        vb[x] = jnp.broadcast_to(weights[x:x + 1, :], (CB, cols)).astype(jnp.bfloat16)

    def ra_block(b, carry):
        ra_up(b).wait_recv()
        ra_dn(b).wait_recv()
        before = z_before[b].astype(jnp.float32)
        ps[b, rows8 * CB:(rows8 + RMAX) * CB, :] = before.reshape(RMAX * CB, cols)
        after = z_after[b].astype(jnp.float32)
        ps[b, (rows8 + RMAX) * CB:used * CB, :] = after.reshape(RMAX * CB, cols)
        for c in range(CB):
            rr = radii_ref[b * CB + c]
            column = ps[b, pl.ds(c, ext, stride=CB), :].astype(jnp.bfloat16)
            os[pl.ds(c, rows8, stride=CB), :] = jnp.dot(
                tab_ra[rr], column, preferred_element_type=jnp.float32
            )
        smooth = os[0:rows * CB, :].reshape(rows, CB, cols).astype(jnp.bfloat16)
        out_ref[:, pl.ds(pl.multiple_of(b * CB, CB), CB), :] = smooth
        mine[b] = smooth * vb[...]
        to_twin(b).start()
        return carry

    lax.fori_loop(0, blocks, ra_block, 0)

    def twin_wait(b, carry):
        to_twin(b).wait_recv()
        return carry

    lax.fori_loop(0, blocks, twin_wait, 0)

    acc[...] = jnp.zeros_like(acc)
    steps = 6 if rows % 6 == 0 else (2 if rows % 2 == 0 else 1)

    def gram(i, carry):
        def row(ref, x):
            return ref[:, pl.ds(x, 1), :, :].reshape(chans, cols)

        own = jnp.concatenate([row(mine, i * steps + s) for s in range(steps)], axis=1)
        oth = jnp.concatenate([row(other, i * steps + s) for s in range(steps)], axis=1)
        msk = jnp.concatenate([vb[i * steps + s] for s in range(steps)], axis=1)
        acc[...] += lax.dot_general(
            jnp.concatenate([own, msk], axis=0), jnp.concatenate([own, oth], axis=0),
            (((1,), (1,)), ((), ())), preferred_element_type=jnp.float32,
        )
        return carry

    lax.fori_loop(0, rows // steps, gram, 0)

    count = jnp.sum(weights, keepdims=True)
    aux[...] = jnp.where(iota((8, 2 * chans), 0) == 0, acc[chans:chans + 8, :], count)

    def part_of(p):
        return acc.at[pl.ds(pl.multiple_of(p * share, share), share), :]

    def rs(p, slot):
        return remote(part_of(p), shares.at[slot], s_rs.at[p], r_rs.at[slot], peer_id(p))

    def ag(p, slot):
        mypart = total.at[pl.ds(pl.multiple_of(slot * share, share), share), :]
        return remote(mypart, mypart, s_ag.at[p], r_ag.at[slot], peer_id(p))

    def au(p, slot):
        return remote(aux, aux_all.at[slot], s_aux.at[p], r_aux.at[slot], peer_id(p))

    def reducing(p, body):
        if reducers == peers:
            body()
        else:
            pl.when(p < reducers)(body)

    each_peer(lambda p: reducing(p, lambda: rs(p, rank).start()))
    each_peer(lambda p: au(p, rank).start())
    aux_all[rank] = aux[...]

    def reduce_own():
        shares[rank] = acc[pl.ds(pl.multiple_of(rank * share, share), share), :]
        each_peer(lambda p: rs(rank, p).wait_recv())
        whole = shares[0]
        whole = lax.fori_loop(1, peers, lambda p, t: t + shares[p], whole)
        total[pl.ds(pl.multiple_of(rank * share, share), share), :] = whole
        each_peer(lambda p: ag(p, rank).start())

    reducing(rank, reduce_own)
    each_peer(lambda p: au(p, p).wait_recv())
    sums = lax.fori_loop(1, peers, lambda p, t: t + aux_all[p], aux_all[0])
    count = sums[1:2, 0:1]
    means = sums[0:1, :] / count
    mean_ref[...] = means[:, 0:chans]
    column = jnp.transpose(jnp.broadcast_to(means[:, 0:chans], (chans, chans)))
    each_peer(lambda p: reducing(p, lambda: ag(p, p).wait_recv()))
    for k in range(2):
        across = means[:, k * chans:(k + 1) * chans]
        block = (total[:, k * chans:(k + 1) * chans] - count * column * across) / (count - 1.0)
        place = band if k == 0 else 1 - band
        cov_ref[pl.ds(pl.multiple_of(place * chans, chans), chans), :] = jnp.transpose(block)

    def finish(b, carry):
        pl.when(has_hi)(lambda: dec_up(b).wait_send())
        pl.when(has_lo)(lambda: dec_dn(b).wait_send())
        ra_up(b).wait_send()
        ra_dn(b).wait_send()
        to_twin(b).wait_send()
        return carry

    lax.fori_loop(0, blocks, finish, 0)
    each_peer(lambda p: reducing(p, lambda: rs(p, rank).wait_send()))
    each_peer(lambda p: au(p, rank).wait_send())
    reducing(rank, lambda: each_peer(lambda p: ag(p, rank).wait_send()))


def per_device(n_ra, n_dec, sky_maps, radii, valid):
    chans, rows, cols = sky_maps.shape
    blocks = chans // CB
    rows8 = up(rows, 16)
    groups = cols // WIDE
    per = -(-rows // groups)
    peers = n_ra * n_dec
    share = chans // min(peers, chans // 8)
    tall = max(per * groups, rows8)
    f32, b16, dma = jnp.float32, jnp.bfloat16, pltpu.SemaphoreType.DMA
    vmem = pl.BlockSpec(memory_space=pltpu.VMEM)
    flat = jnp.transpose(sky_maps, (1, 0, 2))
    packed = pltpu.VMEM((blocks, per, CB, cols), b16)
    edge = pltpu.VMEM((blocks, RMAX, CB, cols), b16)
    smoothed, mean, cov = pl.pallas_call(
        functools.partial(kernel, (n_ra, n_dec, rows, chans, cols)),
        out_shape=(
            jax.ShapeDtypeStruct((rows, chans, cols), b16),
            jax.ShapeDtypeStruct((1, chans), f32),
            jax.ShapeDtypeStruct((2 * chans, chans), f32),
        ),
        in_specs=[pl.BlockSpec(memory_space=pltpu.SMEM), vmem, vmem],
        out_specs=(vmem, vmem, vmem),
        scratch_shapes=[
            pltpu.VMEM((RMAX + 1, 2 * cols, cols), b16),
            pltpu.VMEM((RMAX + 1, rows8, 128), b16),
            pltpu.VMEM((tall * CB, cols), f32),
            pltpu.VMEM((tall * CB, cols), f32),
            pltpu.VMEM((rows8 * CB, cols), f32),
            pltpu.VMEM((blocks, 128 * CB, cols), f32),
            pltpu.VMEM((rows, CB, cols), b16),
            pltpu.VMEM((blocks, rows, CB, cols), b16),
            pltpu.VMEM((blocks, rows, CB, cols), b16),
            packed, packed, packed, packed,
            edge, edge, edge, edge,
            pltpu.VMEM((chans + CB, 2 * chans), f32),
            pltpu.VMEM((peers, share, 2 * chans), f32),
            pltpu.VMEM((chans, 2 * chans), f32),
            pltpu.VMEM((8, 2 * chans), f32),
            pltpu.VMEM((peers, 8, 2 * chans), f32),
            dma((2, blocks)), dma((2, blocks)), dma((2, blocks)), dma((2, blocks)),
            dma((blocks,)), dma((blocks,)),
            dma((peers,)), dma((peers,)), dma((peers,)), dma((peers,)), dma((peers,)), dma((peers,)),
        ],
        compiler_params=pltpu.CompilerParams(
            collective_id=0, has_side_effects=True, vmem_limit_bytes=52 * 1024 * 1024
        ),
    )(radii, flat, valid)
    return (jnp.transpose(smoothed, (1, 0, 2)), mean.reshape(chans), cov)


def solution(mesh):
    return jax.shard_map(
        functools.partial(per_device, mesh.shape["ra"], mesh.shape["dec"]),
        mesh=mesh,
        in_specs=(
            P(("groups", "band"), "ra", "dec"),
            P(("groups", "band")),
            P(("groups", "ra"), "dec"),
        ),
        out_specs=(P(("groups", "band"), "ra", "dec"), P(("groups", "band")), P("groups", "band")),
        check_vma=False,
    )
```

time: 191 us -> 63 us (0.33)
  waiting for transfers between devices: 82.4 us -> 0 us
  Pallas kernels: 0 us -> 56 us
  blocking collectives: 22.4 us -> 0 us
  local copies, waits for them, and re-layouts: 26.6 us -> 6.1 us
  other arithmetic: 18.3 us -> 0 us
  matrix products: 16.2 us -> 0 us
  between operations: 14.7 us -> 0.65 us
  starting transfers between devices: 10.1 us -> 0 us
    pallas_call x0 -> x1, Pallas kernels: none -> 56 us  [per_device(): pl.pallas_call(functools.partial(kernel, (n_ra, n_dec, rows, chans, cols)...]
    psum x1 -> x0, waiting for transfers between devices: 43.8 us -> none  [per_device(): sums, count, block = lax.psum((sums, count, block), ('ra', 'dec'))]
    ppermute x4 -> x0, waiting for transfers between devices: 25.3 us -> none  [the longest x2 14 us: extended(): before = lax.ppermute(last, axis, up)]
    psum x1 -> x0, blocking collectives: 22.4 us -> none  [per_device(): sums, count, block = lax.psum((sums, count, block), ('ra', 'dec'))]
    dot_general x2 -> x0, matrix products: 16.2 us -> none  [the longest x1 13.9 us: per_device(): jnp.einsum('czy,czw->cwy', across, ra_band, preferred_element_type=jnp.fl...]
    all_gather x1 -> x0, waiting for transfers between devices: 13.3 us -> none  [per_device(): every = lax.all_gather(smoothed, 'band', axis=0, tiled=True)]
    ppermute x4 -> x0, starting transfers between devices: 9.89 us -> none  [the longest x2 6.5 us: extended(): before = lax.ppermute(last, axis, up)]
    ppermute x4 -> x0, local copies, waits for them, and re-layouts: 8.28 us -> none  [the longest x2 4.53 us: extended(): after = lax.ppermute(initial, axis, down)]
  transfers between devices with their start and end apart: 6 -> 0, of which waited for: 6 -> 0; matrix products, arithmetic and copies ran while one was open for 9% -> 0% of each run, Pallas kernels for 0% -> 0%
where the time goes in v1:
time: 63 us; the launch traced here: 62.7 us
  Pallas kernels  56 us (89%)
  local copies, waits for them, and re-layouts  6.1 us (10%)
  between operations  0.65 us (1%)
    pallas_call x1, Pallas kernels, per_device(): pl.pallas_call(functools.partial(kernel, (n_ra, n_dec, rows, chans, cols)...  56 us
    unnamed x7, local copies, waits for them, and re-layouts  6.1 us

profile of v1, /device:TPU:0, one launch (start us, length us, event | category | flops | bytes accessed | tf_op | source)
XLA Modules:
  0.0 62.7 jit_solution(15199844914399065137)
XLA Ops:
  0.6 0.0 copy-start
  0.6 0.8 %copy-done = s32[78,128]{1,0:T(8,128)S(1)} copy-done((s32[78,128]{1,0:T(8,128)S(1)}, s32[78,128]{1,0:T(8,128)}, u32[]{:S(2)}) %copy-start) | copy-done | bytes 39960
  1.4 0.0 copy-start.1
  1.4 0.7 %copy-done.1 = s32[128]{0:T(128)S(1)} copy-done((s32[128]{0:T(128)S(1)}, s32[128]{0:T(128)}, u32[]{:S(2)}) %copy-start.1) | copy-done | bytes 536
  2.1 56.0 %shard_map.58 = (bf16[78,128,128]{2,1,0:T(8,128)(2,1)}, f32[1,128]{1,0:T(1,128)S(1)}, f32[256,128]{1,0:T(8,128)S(1)}) custom-call(s32[128]{0:T(128)S(1)} %copy-done.1, bf16[78,128,128]{2,1,0:T(8,128)(2,1)} %bitcast.4, s32[78,128]{1,0:T(8,128)S(1)} %copy-done), custom_call_target="tpu_custom_call" | custom-call | tf_op jit(solution)/shard_map/pallas_call | solution.py:312
  58.1 3.5 %copy.9 = bf16[128,78,128]{2,0,1:T(8,128)(2,1)} copy(bf16[128,78,128]{2,0,1:T(8,128)(2,1)} %bitcast.5) | data formatting | bytes 5111808
  61.6 0.5 copy.10
  62.1 0.7 %copy.11 = f32[256,128]{1,0:T(8,128)} copy(f32[256,128]{1,0:T(8,128)S(1)} %get-tuple-element.14) | data formatting | bytes 262144
Async XLA Ops:
  0.6 0.8 %copy-start = (s32[78,128]{1,0:T(8,128)S(1)}, s32[78,128]{1,0:T(8,128)}, u32[]{:S(2)}) copy-start(s32[78,128]{1,0:T(8,128)} %valid_ref.1) | copy-start | bytes 119812
  1.4 0.7 %copy-start.1 = (s32[128]{0:T(128)S(1)}, s32[128]{0:T(128)}, u32[]{:S(2)}) copy-start(s32[128]{0:T(128)} %radii_ref.1) | copy-start | bytes 1540

commit v2 on v1

--- a/solution.py
+++ b/solution.py
@@ -21,9 +21,16 @@
     return lax.broadcasted_iota(jnp.int32, shape, dim)
 
 
+def inner_rows(rows):
+    first = RMAX // 16 * 16
+    last = up(rows - RMAX, 16)
+    return first, last - first, up(RMAX, 8)
+
+
 def kernel(
-    dims, radii_ref, sky_ref, valid_ref, out_ref, mean_ref, cov_ref,
-    tab_dec, tab_ra, xs, hs, os, ps, vb, mine, other,
+    dims, radii_ref, sky_hbm, valid_hbm, out_ref, mean_ref, cov_ref,
+    sky_ref, valid_ref, loads,
+    tab_dec, tab_in, tab_ed, xs, hs, os, ps, vb, mine_in, mine_ed, other_in, other_ed,
     pack_up, pack_dn, halo_lo, halo_hi, edge_lo, edge_hi, z_before, z_after,
     acc, shares, total, aux, aux_all,
     s_dec, r_dec, s_ra, r_ra, s_band, r_band, s_rs, r_rs, s_ag, r_ag, s_aux, r_aux,
@@ -37,6 +44,7 @@
     reducers = min(peers, chans // 8)
     share = chans // reducers
     ext = 128
+    in_at, in_rows, edge_rows = inner_rows(rows)
     ra, dec, band = lax.axis_index("ra"), lax.axis_index("dec"), lax.axis_index("band")
     rank = ra * n_dec + dec
     nxt, prv = lax.rem(ra + 1, n_ra), lax.rem(ra + n_ra - 1, n_ra)
@@ -51,9 +59,31 @@
             return carry
         lax.fori_loop(1, peers, step, 0)
 
+    def table(r, carry):
+        radius = r.astype(jnp.float32)
+        spread = 0.5 * radius
+        k = lax.rem(iota((8, cols), 0) - iota((8, cols), 1) + cols + cols // 2, cols) - cols // 2
+        k = k.astype(jnp.float32)
+        raw = jnp.where(jnp.abs(k) <= radius, jnp.exp(-(k * k) / (2.0 * spread * spread)), 0.0)
+        first = raw / jnp.sum(raw, axis=1, keepdims=True)
+        full = jnp.concatenate([pltpu.roll(first, 8 * t, 1) for t in range(cols // 8)], axis=0)
+        near = jnp.abs(iota((cols, cols), 0) - iota((cols, cols), 1)) <= cols // 2
+        tab_in[r] = full[in_at:in_at + in_rows].astype(jnp.bfloat16)
+        ends = jnp.concatenate([full[0:edge_rows], full[rows8 - edge_rows:rows8]], axis=0)
+        tab_ed[r] = ends.astype(jnp.bfloat16)
+        tab_dec[r, 0:cols, :] = jnp.where(near, full, 0.0).astype(jnp.bfloat16)
+        tab_dec[r, cols:2 * cols, :] = jnp.where(near, 0.0, full).astype(jnp.bfloat16)
+        return carry
+
+    load_sky = pltpu.make_async_copy(sky_hbm, sky_ref, loads.at[0])
+    load_valid = pltpu.make_async_copy(valid_hbm, valid_ref, loads.at[1])
+    load_sky.start()
+    load_valid.start()
     barrier = pltpu.get_barrier_semaphore()
     each_peer(lambda p: pl.semaphore_signal(barrier, inc=1, device_id=peer_id(p), device_id_type=MESH))
     pl.semaphore_signal(barrier, inc=1, device_id=twin, device_id_type=MESH)
+    lax.fori_loop(1, RMAX + 1, table, 0)
+    load_sky.wait()
     pl.semaphore_wait(barrier, peers)
 
     def remote(src, dst, send, recv, target):
@@ -73,26 +103,34 @@
     def ra_dn(b):
         return remote(edge_lo.at[b], z_after.at[b], s_ra.at[1, b], r_ra.at[1, b], {"ra": prv})
 
-    def to_twin(b):
-        return remote(mine.at[b], other.at[b], s_band.at[b], r_band.at[b], twin)
+    def to_twin(k, b):
+        mine, other = ((mine_ed, other_ed), (mine_in, other_in))[k]
+        return remote(mine.at[b], other.at[b], s_band.at[k, b], r_band.at[k, b], twin)
 
     has_hi, has_lo = dec < n_dec - 1, dec > 0
     lanes = iota((1, 1, cols), 2)
+    inner = rows - 2 * RMAX
+    order = [*range(RMAX), *range(rows - RMAX, rows), *range(RMAX, rows - RMAX)]
     tall = per * groups
     xs[...] = jnp.zeros_like(xs)
+    hs[...] = jnp.zeros_like(hs)
 
     def load_block(b):
         at = pl.multiple_of(b * CB, CB)
         block = sky_ref[:, pl.ds(at, CB), :].astype(jnp.float32)
         xs[0:rows * CB, :] = block.reshape(rows * CB, cols)
 
-    def pack_block(b, carry):
-        load_block(b)
+    def pack_block(b):
+        at = pl.multiple_of(b * CB, CB)
 
         def packed(first):
             result = jnp.zeros((per, CB, cols), jnp.float32)
             for g in range(groups):
-                part = xs[g * per * CB:(g + 1) * per * CB, :].reshape(per, CB, cols)
+                end = min(rows, (g + 1) * per)
+                part = sky_ref[g * per:end, pl.ds(at, CB), :].astype(jnp.float32)
+                if end < (g + 1) * per:
+                    fill = jnp.zeros(((g + 1) * per - end, CB, cols), jnp.float32)
+                    part = jnp.concatenate([part, fill], axis=0)
                 turned = pltpu.roll(part, (WIDE * g - first) % cols, 2)
                 inside = (lanes >= WIDE * g) & (lanes < WIDE * (g + 1))
                 result = jnp.where(inside, turned, result)
@@ -108,49 +146,75 @@
             pack_dn[b] = packed(0)
             dec_dn(b).start()
 
-        return carry
-
-    lax.fori_loop(0, blocks, pack_block, 0)
-
-    def table(r, carry):
-        radius = r.astype(jnp.float32)
-        spread = 0.5 * radius
-
-        def taps(k):
-            k = k.astype(jnp.float32)
-            return jnp.where(jnp.abs(k) <= radius, jnp.exp(-(k * k) / (2.0 * spread * spread)), 0.0)
-
-        norm = jnp.sum(taps(iota((1, 128), 1) - 64), axis=1, keepdims=True)
-        z, y = iota((cols, cols), 0), iota((cols, cols), 1)
-        tab_dec[r, 0:cols, :] = (taps(z - y) / norm).astype(jnp.bfloat16)
-        j = jnp.where(z < WIDE, cols + z, jnp.where((z >= 64) & (z < 64 + WIDE), z - 64 - WIDE, 4 * cols))
-        tab_dec[r, cols:2 * cols, :] = (taps(j - y) / norm).astype(jnp.bfloat16)
-        x, e = iota((rows8, ext), 0), iota((rows8, ext), 1)
-        at = jnp.where(
-            e < rows, e,
-            jnp.where(
-                (e >= rows8) & (e < rows8 + RMAX), e - rows8 - RMAX,
-                jnp.where((e >= rows8 + RMAX) & (e < rows8 + 2 * RMAX), e - rows8 - RMAX + rows, 4 * ext),
-            ),
-        )
-        tab_ra[r] = (taps(at - x) / norm).astype(jnp.bfloat16)
-        return carry
-
-    lax.fori_loop(1, RMAX + 1, table, 0)
-
-    used = rows8 + 2 * RMAX
-
-    @pl.when(jnp.logical_not(has_lo))
-    def _():
-        halo_lo[...] = jnp.zeros_like(halo_lo)
-
-    @pl.when(jnp.logical_not(has_hi))
-    def _():
-        halo_hi[...] = jnp.zeros_like(halo_hi)
+    ahead = min(2, blocks)
+    for b in range(ahead):
+        pack_block(jnp.int32(b))
+
+    load_valid.wait()
+    weights = valid_ref[...].astype(jnp.float32)
+    for at, x in enumerate(order):
+        vb[at] = jnp.broadcast_to(weights[x:x + 1, :], (CB, cols)).astype(jnp.bfloat16)
+
+    def unpack(b, side):
+        low = None if side == "high" else halo_lo[b].astype(jnp.float32)
+        high = None if side == "low" else halo_hi[b].astype(jnp.float32)
+        for g in range(groups):
+            if side != "high":
+                left = pltpu.roll(low, (cols - WIDE - WIDE * g) % cols, 2)
+            if side != "low":
+                right = pltpu.roll(high, (-WIDE * g) % cols, 2)
+            on_right = lanes < cols // 2
+            if side == "both":
+                both = jnp.where(on_right, right, left)
+            elif side == "low":
+                both = jnp.where(on_right, 0.0, left)
+            else:
+                both = jnp.where(on_right, right, 0.0)
+            hs[g * per * CB:(g + 1) * per * CB, :] = both.reshape(per * CB, cols)
+
+    def for_blocks(body):
+        def step(b, carry):
+            body(b)
+            return carry
+        lax.fori_loop(0, blocks, step, 0)
+
+    def smooth_rows(b, tab, height):
+        for c in range(CB):
+            rr = radii_ref[b * CB + c]
+            column = ps[b, pl.ds(c, ext, stride=CB), :].astype(jnp.bfloat16)
+            os[pl.ds(c, height, stride=CB), :] = jnp.dot(
+                tab[rr], column, preferred_element_type=jnp.float32
+            )
+
+    def gram_of(mine, other, first, height):
+        steps = next(n for n in (8, 6, 4, 2, 1) if height % n == 0)
+        if height % 34 == 0:
+            steps = 34
+        if height % 22 == 0:
+            steps = 22
+
+        def gram(i, carry):
+            def row(ref, x):
+                return ref[:, pl.ds(x, 1), :, :].reshape(chans, cols)
+
+            own = jnp.concatenate([row(mine, i * steps + s) for s in range(steps)], axis=1)
+            oth = jnp.concatenate([row(other, i * steps + s) for s in range(steps)], axis=1)
+            msk = jnp.concatenate([vb[first + i * steps + s] for s in range(steps)], axis=1)
+            acc[...] += lax.dot_general(
+                jnp.concatenate([own, msk], axis=0), jnp.concatenate([own, oth], axis=0),
+                (((1,), (1,)), ((), ())), preferred_element_type=jnp.float32,
+            )
+            return carry
+
+        lax.fori_loop(0, height // steps, gram, 0)
 
     def dec_block(b, carry):
+        @pl.when(b + ahead < blocks)
+        def _():
+            pack_block(b + ahead)
+
         load_block(b)
-        ps[b, used * CB:ext * CB, :] = jnp.zeros(((ext - used) * CB, cols), jnp.float32)
+        ps[b, rows8 * CB:ext * CB, :] = jnp.zeros(((ext - rows8) * CB, cols), jnp.float32)
 
         @pl.when(has_lo)
         def _():
@@ -160,13 +224,18 @@
         def _():
             dec_dn(b).wait_recv()
 
-        low = halo_lo[b].astype(jnp.float32)
-        high = halo_hi[b].astype(jnp.float32)
-        for g in range(groups):
-            left = pltpu.roll(low, (64 - WIDE * g) % cols, 2)
-            right = pltpu.roll(high, (-WIDE * g) % cols, 2)
-            both = jnp.where(lanes < 64, right, left)
-            hs[g * per * CB:(g + 1) * per * CB, :] = both.reshape(per * CB, cols)
+        @pl.when(has_lo & has_hi)
+        def _():
+            unpack(b, "both")
+
+        @pl.when(has_lo & jnp.logical_not(has_hi))
+        def _():
+            unpack(b, "low")
+
+        @pl.when(has_hi & jnp.logical_not(has_lo))
+        def _():
+            unpack(b, "high")
+
         for c in range(CB):
             rr = radii_ref[b * CB + c]
             main = xs[pl.ds(c, rows8, stride=CB), :]
@@ -180,59 +249,41 @@
         edge_hi[b] = last.reshape(RMAX, CB, cols).astype(jnp.bfloat16)
         ra_up(b).start()
         ra_dn(b).start()
+        smooth_rows(b, tab_in, in_rows)
+        at = RMAX - in_at
+        smooth = os[at * CB:(at + inner) * CB, :].reshape(inner, CB, cols).astype(jnp.bfloat16)
+        out_ref[RMAX:rows - RMAX, pl.ds(pl.multiple_of(b * CB, CB), CB), :] = smooth
+        mine_in[b] = smooth * vb[2 * RMAX:rows]
+        to_twin(1, b).start()
         return carry
 
     lax.fori_loop(0, blocks, dec_block, 0)
-
-    weights = valid_ref[...].astype(jnp.float32)
-    for x in range(rows):
-        vb[x] = jnp.broadcast_to(weights[x:x + 1, :], (CB, cols)).astype(jnp.bfloat16)
+    for_blocks(lambda b: to_twin(1, b).wait_recv())
+    acc[...] = jnp.zeros_like(acc)
+    gram_of(mine_in, other_in, 2 * RMAX, inner)
 
     def ra_block(b, carry):
         ra_up(b).wait_recv()
         ra_dn(b).wait_recv()
         before = z_before[b].astype(jnp.float32)
-        ps[b, rows8 * CB:(rows8 + RMAX) * CB, :] = before.reshape(RMAX * CB, cols)
+        ps[b, (ext - RMAX) * CB:ext * CB, :] = before.reshape(RMAX * CB, cols)
         after = z_after[b].astype(jnp.float32)
-        ps[b, (rows8 + RMAX) * CB:used * CB, :] = after.reshape(RMAX * CB, cols)
-        for c in range(CB):
-            rr = radii_ref[b * CB + c]
-            column = ps[b, pl.ds(c, ext, stride=CB), :].astype(jnp.bfloat16)
-            os[pl.ds(c, rows8, stride=CB), :] = jnp.dot(
-                tab_ra[rr], column, preferred_element_type=jnp.float32
-            )
-        smooth = os[0:rows * CB, :].reshape(rows, CB, cols).astype(jnp.bfloat16)
-        out_ref[:, pl.ds(pl.multiple_of(b * CB, CB), CB), :] = smooth
-        mine[b] = smooth * vb[...]
-        to_twin(b).start()
+        ps[b, rows * CB:(rows + RMAX) * CB, :] = after.reshape(RMAX * CB, cols)
+        smooth_rows(b, tab_ed, 2 * edge_rows)
+        low = os[0:RMAX * CB, :].reshape(RMAX, CB, cols).astype(jnp.bfloat16)
+        at = 2 * edge_rows - rows8 + rows - RMAX
+        high = os[at * CB:(at + RMAX) * CB, :].reshape(RMAX, CB, cols).astype(jnp.bfloat16)
+        here = pl.ds(pl.multiple_of(b * CB, CB), CB)
+        out_ref[0:RMAX, here, :] = low
+        out_ref[rows - RMAX:rows, here, :] = high
+        mine_ed[b, 0:RMAX] = low * vb[0:RMAX]
+        mine_ed[b, RMAX:2 * RMAX] = high * vb[RMAX:2 * RMAX]
+        to_twin(0, b).start()
         return carry
 
     lax.fori_loop(0, blocks, ra_block, 0)
-
-    def twin_wait(b, carry):
-        to_twin(b).wait_recv()
-        return carry
-
-    lax.fori_loop(0, blocks, twin_wait, 0)
-
-    acc[...] = jnp.zeros_like(acc)
-    steps = 6 if rows % 6 == 0 else (2 if rows % 2 == 0 else 1)
-
-    def gram(i, carry):
-        def row(ref, x):
-            return ref[:, pl.ds(x, 1), :, :].reshape(chans, cols)
-
-        own = jnp.concatenate([row(mine, i * steps + s) for s in range(steps)], axis=1)
-        oth = jnp.concatenate([row(other, i * steps + s) for s in range(steps)], axis=1)
-        msk = jnp.concatenate([vb[i * steps + s] for s in range(steps)], axis=1)
-        acc[...] += lax.dot_general(
-            jnp.concatenate([own, msk], axis=0), jnp.concatenate([own, oth], axis=0),
-            (((1,), (1,)), ((), ())), preferred_element_type=jnp.float32,
-        )
-        return carry
-
-    lax.fori_loop(0, rows // steps, gram, 0)
-
+    for_blocks(lambda b: to_twin(0, b).wait_recv())
+    gram_of(mine_ed, other_ed, 0, 2 * RMAX)
     count = jnp.sum(weights, keepdims=True)
     aux[...] = jnp.where(iota((8, 2 * chans), 0) == 0, acc[chans:chans + 8, :], count)
 
@@ -286,7 +337,8 @@
         pl.when(has_lo)(lambda: dec_dn(b).wait_send())
         ra_up(b).wait_send()
         ra_dn(b).wait_send()
-        to_twin(b).wait_send()
+        to_twin(0, b).wait_send()
+        to_twin(1, b).wait_send()
         return carry
 
     lax.fori_loop(0, blocks, finish, 0)
@@ -306,6 +358,9 @@
     tall = max(per * groups, rows8)
     f32, b16, dma = jnp.float32, jnp.bfloat16, pltpu.SemaphoreType.DMA
     vmem = pl.BlockSpec(memory_space=pltpu.VMEM)
+    hbm = pl.BlockSpec(memory_space=pltpu.HBM)
+    in_at, in_rows, edge_rows = inner_rows(rows)
+    inner, outer = rows - 2 * RMAX, 2 * RMAX
     flat = jnp.transpose(sky_maps, (1, 0, 2))
     packed = pltpu.VMEM((blocks, per, CB, cols), b16)
     edge = pltpu.VMEM((blocks, RMAX, CB, cols), b16)
@@ -316,18 +371,24 @@
             jax.ShapeDtypeStruct((1, chans), f32),
             jax.ShapeDtypeStruct((2 * chans, chans), f32),
         ),
-        in_specs=[pl.BlockSpec(memory_space=pltpu.SMEM), vmem, vmem],
+        in_specs=[pl.BlockSpec(memory_space=pltpu.SMEM), hbm, hbm],
         out_specs=(vmem, vmem, vmem),
         scratch_shapes=[
+            pltpu.VMEM((rows, chans, cols), b16),
+            pltpu.VMEM((rows, cols), jnp.int32),
+            dma((2,)),
             pltpu.VMEM((RMAX + 1, 2 * cols, cols), b16),
-            pltpu.VMEM((RMAX + 1, rows8, 128), b16),
+            pltpu.VMEM((RMAX + 1, in_rows, 128), b16),
+            pltpu.VMEM((RMAX + 1, 2 * edge_rows, 128), b16),
             pltpu.VMEM((tall * CB, cols), f32),
             pltpu.VMEM((tall * CB, cols), f32),
             pltpu.VMEM((rows8 * CB, cols), f32),
             pltpu.VMEM((blocks, 128 * CB, cols), f32),
             pltpu.VMEM((rows, CB, cols), b16),
-            pltpu.VMEM((blocks, rows, CB, cols), b16),
-            pltpu.VMEM((blocks, rows, CB, cols), b16),
+            pltpu.VMEM((blocks, inner, CB, cols), b16),
+            pltpu.VMEM((blocks, outer, CB, cols), b16),
+            pltpu.VMEM((blocks, inner, CB, cols), b16),
+            pltpu.VMEM((blocks, outer, CB, cols), b16),
             packed, packed, packed, packed,
             edge, edge, edge, edge,
             pltpu.VMEM((chans + CB, 2 * chans), f32),
@@ -336,11 +397,11 @@
             pltpu.VMEM((8, 2 * chans), f32),
             pltpu.VMEM((peers, 8, 2 * chans), f32),
             dma((2, blocks)), dma((2, blocks)), dma((2, blocks)), dma((2, blocks)),
-            dma((blocks,)), dma((blocks,)),
+            dma((2, blocks)), dma((2, blocks)),
             dma((peers,)), dma((peers,)), dma((peers,)), dma((peers,)), dma((peers,)), dma((peers,)),
         ],
         compiler_params=pltpu.CompilerParams(
-            collective_id=0, has_side_effects=True, vmem_limit_bytes=52 * 1024 * 1024
+            collective_id=0, has_side_effects=True, vmem_limit_bytes=32 * 1024 * 1024
         ),
     )(radii, flat, valid)
     return (jnp.transpose(smoothed, (1, 0, 2)), mean.reshape(chans), cov)

time: 63 us -> 56.6 us (0.90)
  Pallas kernels: 56 us -> 50.1 us
    pallas_call x1, Pallas kernels: 56 us -> 50.1 us  [per_device(): pl.pallas_call(functools.partial(kernel, (n_ra, n_dec, rows, chans, cols)...]
    unnamed x7 -> x9, local copies, waits for them, and re-layouts: 6.1 us -> 5.79 us
where the time goes in v2:
time: 56.6 us; the launch traced here: 56.5 us
  Pallas kernels  50.1 us (89%)
  local copies, waits for them, and re-layouts  5.79 us (10%)
  between operations  0.65 us (1%)
    pallas_call x1, Pallas kernels, per_device(): pl.pallas_call(functools.partial(kernel, (n_ra, n_dec, rows, chans, cols)...  50.1 us
    unnamed x9, local copies, waits for them, and re-layouts  5.79 us

profile of v2, /device:TPU:0, one launch (start us, length us, event | category | flops | bytes accessed | tf_op | source)
XLA Modules:
  0.0 56.5 jit_solution(5631129201603299532)
XLA Ops:
  0.6 0.0 copy-start
  0.6 1.7 %copy-done = bf16[128,78,128]{2,0,1:T(8,128)(2,1)S(1)} copy-done((bf16[128,78,128]{2,0,1:T(8,128)(2,1)S(1)}, bf16[128,78,128]{2,0,1:T(8,128)(2,1)}, u32[]{:S(2)}) %copy-start) | copy-done | bytes 2555928
  2.4 0.0 copy-start.1
  2.4 0.8 %copy-done.1 = s32[78,128]{1,0:T(8,128)S(1)} copy-done((s32[78,128]{1,0:T(8,128)S(1)}, s32[78,128]{1,0:T(8,128)}, u32[]{:S(2)}) %copy-start.1) | copy-done | bytes 39960
  3.1 0.0 copy-start.2
  3.1 0.7 %copy-done.2 = s32[128]{0:T(128)S(1)} copy-done((s32[128]{0:T(128)S(1)}, s32[128]{0:T(128)}, u32[]{:S(2)}) %copy-start.2) | copy-done | bytes 536
  3.8 50.1 %shard_map.58 = (bf16[78,128,128]{2,1,0:T(8,128)(2,1)S(1)}, f32[1,128]{1,0:T(1,128)S(1)}, f32[256,128]{1,0:T(8,128)S(1)}) custom-call(s32[128]{0:T(128)S(1)} %copy-done.2, bf16[78,128,128]{2,1,0:T(8,128)(2,1)S(1)} %bitcast.3, s32[78,128]{1,0:T(8,128)S(1)} %copy-done.1), custom_call_target="tpu_custom_call" | custom-call | tf_op jit(solution)/shard_map/pallas_call | solution.py:367
  53.9 1.5 %copy.9 = bf16[128,78,128]{2,0,1:T(8,128)(2,1)} copy(bf16[128,78,128]{2,0,1:T(8,128)(2,1)S(1)} %bitcast.4) | data formatting | bytes 5111808
  55.3 0.5 copy.10
  55.9 0.7 %copy.11 = f32[256,128]{1,0:T(8,128)} copy(f32[256,128]{1,0:T(8,128)S(1)} %get-tuple-element.14) | data formatting | bytes 262144
Async XLA Ops:
  0.6 1.7 %copy-start = (bf16[128,78,128]{2,0,1:T(8,128)(2,1)S(1)}, bf16[128,78,128]{2,0,1:T(8,128)(2,1)}, u32[]{:S(2)}) copy-start(bf16[128,78,128]{2,0,1:T(8,128)(2,1)} %param.3) | copy-start | bytes 7667716
  2.4 0.8 %copy-start.1 = (s32[78,128]{1,0:T(8,128)S(1)}, s32[78,128]{1,0:T(8,128)}, u32[]{:S(2)}) copy-start(s32[78,128]{1,0:T(8,128)} %valid_hbm.1) | copy-start | bytes 119812
  3.1 0.7 %copy-start.2 = (s32[128]{0:T(128)S(1)}, s32[128]{0:T(128)}, u32[]{:S(2)}) copy-start(s32[128]{0:T(128)} %radii_ref.1) | copy-start | bytes 1540

commit v3 on v2

--- a/solution.py
+++ b/solution.py
@@ -249,15 +249,18 @@
         edge_hi[b] = last.reshape(RMAX, CB, cols).astype(jnp.bfloat16)
         ra_up(b).start()
         ra_dn(b).start()
+        return carry
+
+    def inner_block(b):
         smooth_rows(b, tab_in, in_rows)
         at = RMAX - in_at
         smooth = os[at * CB:(at + inner) * CB, :].reshape(inner, CB, cols).astype(jnp.bfloat16)
         out_ref[RMAX:rows - RMAX, pl.ds(pl.multiple_of(b * CB, CB), CB), :] = smooth
         mine_in[b] = smooth * vb[2 * RMAX:rows]
         to_twin(1, b).start()
-        return carry
 
     lax.fori_loop(0, blocks, dec_block, 0)
+    for_blocks(inner_block)
     for_blocks(lambda b: to_twin(1, b).wait_recv())
     acc[...] = jnp.zeros_like(acc)
     gram_of(mine_in, other_in, 2 * RMAX, inner)

time: 56.6 us -> 56.7 us (level)
  no operation moved by 1% of the time
where the time goes in v3:
time: 56.7 us; the launch traced here: 56.5 us
  Pallas kernels  50 us (88%)
  local copies, waits for them, and re-layouts  5.79 us (10%)
  between operations  0.65 us (1%)
    pallas_call x1, Pallas kernels, per_device(): pl.pallas_call(functools.partial(kernel, (n_ra, n_dec, rows, chans, cols)...  50 us
    unnamed x9, local copies, waits for them, and re-layouts  5.79 us

profile of v3, /device:TPU:0, one launch (start us, length us, event | category | flops | bytes accessed | tf_op | source)
XLA Modules:
  0.0 56.5 jit_solution(14351341707061020654)
XLA Ops:
  0.6 0.0 copy-start
  0.6 1.7 %copy-done = bf16[128,78,128]{2,0,1:T(8,128)(2,1)S(1)} copy-done((bf16[128,78,128]{2,0,1:T(8,128)(2,1)S(1)}, bf16[128,78,128]{2,0,1:T(8,128)(2,1)}, u32[]{:S(2)}) %copy-start) | copy-done | bytes 2555928
  2.4 0.0 copy-start.1
  2.4 0.8 %copy-done.1 = s32[78,128]{1,0:T(8,128)S(1)} copy-done((s32[78,128]{1,0:T(8,128)S(1)}, s32[78,128]{1,0:T(8,128)}, u32[]{:S(2)}) %copy-start.1) | copy-done | bytes 39960
  3.1 0.0 copy-start.2
  3.1 0.7 %copy-done.2 = s32[128]{0:T(128)S(1)} copy-done((s32[128]{0:T(128)S(1)}, s32[128]{0:T(128)}, u32[]{:S(2)}) %copy-start.2) | copy-done | bytes 536
  3.8 50.0 %shard_map.58 = (bf16[78,128,128]{2,1,0:T(8,128)(2,1)S(1)}, f32[1,128]{1,0:T(1,128)S(1)}, f32[256,128]{1,0:T(8,128)S(1)}) custom-call(s32[128]{0:T(128)S(1)} %copy-done.2, bf16[78,128,128]{2,1,0:T(8,128)(2,1)S(1)} %bitcast.3, s32[78,128]{1,0:T(8,128)S(1)} %copy-done.1), custom_call_target="tpu_custom_call" | custom-call | tf_op jit(solution)/shard_map/pallas_call | solution.py:370
  53.8 1.5 %copy.9 = bf16[128,78,128]{2,0,1:T(8,128)(2,1)} copy(bf16[128,78,128]{2,0,1:T(8,128)(2,1)S(1)} %bitcast.4) | data formatting | bytes 5111808
  55.3 0.5 copy.10
  55.8 0.7 %copy.11 = f32[256,128]{1,0:T(8,128)} copy(f32[256,128]{1,0:T(8,128)S(1)} %get-tuple-element.14) | data formatting | bytes 262144
Async XLA Ops:
  0.6 1.7 %copy-start = (bf16[128,78,128]{2,0,1:T(8,128)(2,1)S(1)}, bf16[128,78,128]{2,0,1:T(8,128)(2,1)}, u32[]{:S(2)}) copy-start(bf16[128,78,128]{2,0,1:T(8,128)(2,1)} %param.3) | copy-start | bytes 7667716
  2.4 0.8 %copy-start.1 = (s32[78,128]{1,0:T(8,128)S(1)}, s32[78,128]{1,0:T(8,128)}, u32[]{:S(2)}) copy-start(s32[78,128]{1,0:T(8,128)} %valid_hbm.1) | copy-start | bytes 119812
  3.1 0.7 %copy-start.2 = (s32[128]{0:T(128)S(1)}, s32[128]{0:T(128)}, u32[]{:S(2)}) copy-start(s32[128]{0:T(128)} %radii_ref.1) | copy-start | bytes 1540
